TPU v7x, 32 devices: a whole 2x2x4 slice. The times are simulated.
32 devices in a mesh: groups: 2 (over y), tile: 4 (over x, core), cuts: 4 (over z).
Axes of the slice: x: 2, y: 2, z: 4, core: 2. Of those that a mesh axis runs over, the one named last changes fastest.
Arguments:
- trade: bfloat16 [16, 4, 256, 8192], P(('groups', 'cuts'), 'tile'), parts along dimension 0, may hold values from -6 to 6
- factor: bfloat16 [32768, 256], P(('groups', 'tile', 'cuts')), parts along dimension 0, may hold values from -0.375 to 0.375
- scales: float32 [16, 256], P(('groups', 'cuts')), parts along dimension 0, may hold values from 0.1 to 1.9
- core: float32 [512, 256], P('groups'), parts along dimension 0, may hold values from -4 to 4
Outputs:
- grad_factor: float32 [32768, 256], P(('groups', 'tile', 'cuts')), parts along dimension 0
- grad_window: float32 [1024, 256], P(('groups', 'cuts')), parts along dimension 0
- grad_core: float32 [512, 256], P('groups'), parts along dimension 0
- grad_scales: float32 [16, 256], P(('groups', 'cuts')), parts along dimension 0
There are 2 independent parts, one for each index of `groups`. A program takes and returns all parts, laid end to end along the dimension named above; each array names one. Nothing has to cross between parts.
All inputs are finite; a program needn't handle non-finite values.
Results may differ from a plain program's by a relative error of at most 0.00055.
Values may be sent and summed in bfloat16 or wider, within the bound.
A program may use at most 128 MiB of HBM per device.

v0:
```python
import math

import jax
import jax.numpy as jnp
from jax import lax
from jax.sharding import PartitionSpec as P

P_SIZE = 256


def swapped(value, axis, distance):
    mask = 2**distance
    pairs = [(source, source ^ mask) for source in range(lax.axis_size(axis))]
    return lax.ppermute(value, axis, pairs)


def from_root(block, axis, source):
    block = jnp.where(lax.axis_index(axis) == source, block, jnp.zeros_like(block))
    return lax.psum(block, axis)


def body(trade, factor, scales, core):
    n_cuts = lax.axis_size("cuts")
    band_index = lax.axis_index("tile") % 2
    months = trade.shape[0]
    rows_band = trade.shape[2]
    window_size = 2 * rows_band
    highest = lax.Precision.HIGHEST
    own_block = lax.all_gather(factor, "cuts", axis=0, tiled=True)
    block = own_block.shape[0]
    partner_block = swapped(own_block, "tile", 0)
    first_block = jnp.where(band_index == 0, own_block, partner_block)
    second_block = jnp.where(band_index == 0, partner_block, own_block)
    column_factor = jnp.concatenate([first_block, second_block], 0)
    window_block = from_root(own_block, "tile", 0)
    window_rows = lax.dynamic_slice_in_dim(window_block, band_index * rows_band, rows_band, 0)
    window32 = window_rows.astype(jnp.float32)
    coef = 1.0 / math.sqrt(months * n_cuts * window_size)
    acc_columns = jnp.zeros((2 * block, P_SIZE), jnp.float32)
    acc_window = jnp.zeros((rows_band, P_SIZE), jnp.float32)
    acc_core = jnp.zeros((P_SIZE, P_SIZE), jnp.float32)
    diag_terms = []
    for month in range(months):
        diag_k = scales[month]
        inner = diag_k[:, None] * core * diag_k[None, :]
        mapped = jnp.dot(window32, inner, precision=highest).astype(jnp.bfloat16)
        model = lax.dot_general(
            mapped, column_factor, (((1,), (1,)), ((), ())), preferred_element_type=jnp.float32
        )
        residual = (trade[month, 0].astype(jnp.float32) - model).astype(jnp.bfloat16)
        acc_columns = acc_columns + lax.dot_general(
            residual, mapped, (((0,), (0,)), ((), ())), preferred_element_type=jnp.float32
        )
        projected = jnp.dot(residual, column_factor, preferred_element_type=jnp.float32)
        acc_window = acc_window + jnp.dot(projected, inner.T, precision=highest)
        gram = jnp.dot(window32.T, projected, precision=highest)
        acc_core = acc_core + diag_k[:, None] * gram * diag_k[None, :]
        weighted = gram * core
        diag_terms.append(
            jnp.dot(weighted, diag_k, precision=highest)
            + jnp.dot(weighted.T, diag_k, precision=highest)
        )
    diag_stack = jnp.stack(diag_terms, 0)
    halves = acc_columns.reshape(2, block, P_SIZE)
    mine = jnp.where(band_index == 0, halves[0], halves[1])
    other = jnp.where(band_index == 0, halves[1], halves[0])
    received = swapped(other, "tile", 0)
    grad_factor = lax.psum_scatter(mine + received, "cuts", scatter_dimension=0, tiled=True)
    padded = lax.dynamic_update_slice_in_dim(
        jnp.zeros((window_size, P_SIZE), jnp.float32), acc_window, band_index * rows_band, 0
    )
    window_part = lax.psum_scatter(padded, "cuts", scatter_dimension=0, tiled=True)
    window_total = lax.psum(window_part, "tile")
    core_total = lax.psum(acc_core, ("tile", "cuts"))
    diag_total = lax.psum(diag_stack, "tile")
    return (-coef * grad_factor, -coef * window_total, -coef * core_total, -coef * diag_total)


def solution(mesh):
    return jax.shard_map(
        body,
        mesh=mesh,
        in_specs=(
            P(("groups", "cuts"), "tile", None, None),
            P(("groups", "tile", "cuts"), None),
            P(("groups", "cuts"), None),
            P("groups", None),
        ),
        out_specs=(
            P(("groups", "tile", "cuts"), None),
            P(("groups", "cuts"), None),
            P("groups", None),
            P(("groups", "cuts"), None),
        ),
        check_vma=False,
    )
```

profile of v0, /device:TPU:25, one launch (start us, length us, event | category | flops | bytes accessed | tf_op | source)
XLA Modules:
  0.0 382.9 jit_solution(4281532647967686441)
XLA Ops:
  7.9 46.6 %all-gather.2.cloned.1.call-done = bf16[4096,256]{1,0:T(8,128)(2,1)} async-done(((bf16[1024,256]{1,0:T(8,128)(2,1)}), bf16[4096,256]{1,0:T(8,128)(2,1)}) %all-gather.2.cloned.1.call-update) | async-done | bytes 2097168 | tf_op jit(solution)/shard_map/all_gather | solution.py:29
  55.0 4.1 %collective-permute-done = bf16[4096,256]{1,0:T(8,128)(2,1)} collective-permute-done((bf16[4096,256]{1,0:T(8,128)(2,1)}, bf16[4096,256]{1,0:T(8,128)(2,1)}, u32[]{:S(2)}, u32[]{:S(2)}) %collective-permute-start) | collective-permute-done | bytes 2097184 | tf_op jit(solution)/shard_map/ppermute | solution.py:14
  59.1 4.6 %broadcast_select_fusion.2 = (bf16[4096,256]{1,0:T(8,128)(2,1)S(1)}, bf16[4096,256]{1,0:T(8,128)(2,1)}, bf16[4096,256]{1,0:T(8,128)(2,1)}) fusion(bf16[4096,256]{1,0:T(8,128)(2,1)} %all-gather.2.cloned.1.call-done, bf16[4096,256]{1,0:T(8,128)(2,1)} %collective-permute-done, pred[]{:T(512)S(6)} %eq.6, pred[]{:T(512)S(6)} %eq.12), kind=kLoop, calls=%fused_computation.10 | loop fusion | flops 3145728 | bytes 10485762 | tf_op jit(solution)/shard_map/jit(_where)/select_n | solution.py:32
  63.9 52.0 %all-reduce.4.cloned.1.call-done = bf16[4096,256]{1,0:T(8,128)(2,1)} async-done(((bf16[4096,256]{1,0:T(8,128)(2,1)}), bf16[4096,256]{1,0:T(8,128)(2,1)}) %all-reduce.4.cloned.1.call-update) | async-done | bytes 2097168 | tf_op jit(solution)/shard_map/psum | solution.py:19
  115.9 1.3 convolution_convert_fusion.1
  117.2 4.3 %fusion = bf16[256,8192]{1,0:T(8,128)(2,1)S(1)} fusion(bf16[256,256]{1,0:T(8,128)(2,1)S(1)} %convolution_convert_fusion.1, bf16[2,1,256,8192]{3,2,1,0:T(8,128)(2,1)} %param.4, bf16[4096,256]{1,0:T(8,128)(2,1)} %get-tuple-element.5, bf16[4096,256]{1,0:T(8,128)(2,1)S(1)} %get-tuple-element.4), kind=kOutput, calls=%fused_computation.3 | convolution fusion | flops 1088421888 | bytes 12713984 | tf_op jit(solution)/shard_map/dot_general | solution.py:47
  121.4 1.5 convolution_convert_fusion
  122.9 9.6 %fusion.1 = bf16[256,8192]{1,0:T(8,128)(2,1)S(1)} fusion(bf16[256,256]{1,0:T(8,128)(2,1)S(1)} %convolution_convert_fusion, bf16[2,1,256,8192]{3,2,1,0:T(8,128)(2,1)} %param.4, bf16[4096,256]{1,0:T(8,128)(2,1)S(1)} %copy-done.6, bf16[4096,256]{1,0:T(8,128)(2,1)S(1)} %get-tuple-element.4), kind=kOutput, calls=%fused_computation.4 | convolution fusion | flops 1088421888 | bytes 12713984 | tf_op jit(solution)/shard_map/dot_general | solution.py:47
  132.6 1.3 fusion.43
  134.5 1.3 convolution_add_fusion
  135.9 2.8 slice_select_fusion
  138.7 1.6 copy-done
  141.1 4.2 %fusion.41 = f32[256,256]{1,0:T(8,128)S(1)} fusion(bf16[256,8192]{1,0:T(8,128)(2,1)} %copy-done.4, bf16[4096,256]{1,0:T(8,128)(2,1)} %get-tuple-element.5, bf16[4096,256]{1,0:T(8,128)(2,1)S(1)} %get-tuple-element.4), kind=kOutput, calls=%fused_computation.61 | convolution fusion | flops 1082130432 | bytes 8650752 | tf_op jit(solution)/shard_map/dot_general | solution.py:54
  145.9 1.2 fusion.40
  149.7 1.9 multiply_add_fusion
  151.8 14.5 %reduce-scatter.5.cloned.1.call-done = f32[128,256]{1,0:T(8,128)} async-done(((f32[512,256]{1,0:T(8,128)}), f32[128,256]{1,0:T(8,128)}) %reduce-scatter.5.cloned.1.call-update) | async-done | bytes 131088 | tf_op jit(solution)/shard_map/reduce_scatter | solution.py:72
  166.4 7.4 %select_add_fusion = f32[4096,256]{1,0:T(8,128)} fusion(f32[4096,256]{1,0:T(8,128)} %collective-permute-done.1, f32[8192,256]{1,0:T(8,128)} %copy-done, pred[]{:T(512)S(6)} %eq.6), kind=kLoop, calls=%fused_computation.6 | loop fusion | flops 2097152 | bytes 16777216 | tf_op jit(solution)/shard_map/add | solution.py:68
  175.0 6.3 %psum.31 = f32[2,256]{1,0:T(2,128)S(1)} all-reduce(f32[2,256]{1,0:T(2,128)S(1)} %pad_maximum_fusion.1), channel_id=1, replica_groups=mesh['groups'=2,'tile'=4,'cuts'=4] {'tile'}, use_global_device_ids=true, to_apply=%region_5.6 | all-reduce | flops 512 | bytes 4096 | tf_op jit(solution)/shard_map/psum | solution.py:75
  181.9 78.2 %all-reduce.8.cloned.1.call-done = f32[256,256]{1,0:T(8,128)} async-done(((f32[256,256]{1,0:T(8,128)}), f32[256,256]{1,0:T(8,128)}) %all-reduce.8.cloned.1.call-update) | async-done | bytes 262160 | tf_op jit(solution)/shard_map/psum | solution.py:74
  260.0 1.7 broadcast_multiply_fusion.1
  261.7 32.7 %all-reduce.6.cloned.1.call-done = f32[128,256]{1,0:T(8,128)} async-done(((f32[128,256]{1,0:T(8,128)}), f32[128,256]{1,0:T(8,128)}) %all-reduce.6.cloned.1.call-update) | async-done | bytes 131088 | tf_op jit(solution)/shard_map/psum | solution.py:73
  294.4 1.6 broadcast_multiply_fusion.2
  296.0 77.9 %reduce-scatter.3.cloned.1.call-done = f32[1024,256]{1,0:T(8,128)} async-done(((f32[4096,256]{1,0:T(8,128)}), f32[1024,256]{1,0:T(8,128)}) %reduce-scatter.3.cloned.1.call-update) | async-done | bytes 1048592 | tf_op jit(solution)/shard_map/reduce_scatter | solution.py:68
  373.8 2.3 broadcast_multiply_fusion
  (45 shorter events, 7.7 us)
Async XLA Ops:
  7.2 47.4 %all-gather.2.cloned.1.call-start = ((), (), s32[]{:S(2)}) async-start(), calls=%async_computation.2 | async-start | bytes 2621440 | tf_op jit(solution)/shard_map/all_gather | solution.py:29
  7.9 108.0 %all-reduce.4.cloned.1.call-start = ((), (), s32[]{:S(2)}) async-start(), calls=%async_computation.3 | async-start | bytes 4194304 | tf_op jit(solution)/shard_map/psum | solution.py:19
  54.5 4.6 %collective-permute-start = (bf16[4096,256]{1,0:T(8,128)(2,1)}, bf16[4096,256]{1,0:T(8,128)(2,1)}, u32[]{:S(2)}, u32[]{:S(2)}) collective-permute-start(bf16[4096,256]{1,0:T(8,128)(2,1)} %all-gather.2.cloned.1.call-done), channel_id=1, source_target_pairs={{0,4},{4,0},{8,12},{12,8},{1,5},{5,1},{9,13},{13,9},{2,6},{6,2},{1... | collective-permute-start | bytes 6291464 | tf_op jit(solution)/shard_map/ppermute | solution.py:14
  55.0 8.8 %copy-start.8 = (f32[2,256]{1,0:T(2,128)S(1)}, f32[2,256]{1,0:T(2,128)}, u32[]{:S(2)}) copy-start(f32[2,256]{1,0:T(2,128)} %param.6) | copy-start | bytes 6148
  55.0 60.8 %copy-start.1 = (f32[256,256]{1,0:T(8,128)S(1)}, f32[256,256]{1,0:T(8,128)}, u32[]{:S(2)}) copy-start(f32[256,256]{1,0:T(8,128)} %param.7) | copy-start | bytes 786436
  63.8 102.5 %reduce-scatter.5.cloned.1.call-start = ((), (), s32[]{:S(2)}) async-start(), calls=%async_computation.5 | async-start | bytes 655360 | tf_op jit(solution)/shard_map/reduce_scatter | solution.py:72
  117.2 5.8 %copy-start.6 = (bf16[4096,256]{1,0:T(8,128)(2,1)S(1)}, bf16[4096,256]{1,0:T(8,128)(2,1)}, u32[]{:S(2)}) copy-start(bf16[4096,256]{1,0:T(8,128)(2,1)} %get-tuple-element.5) | copy-start | bytes 6291460
  121.4 11.1 %copy-start.4 = (bf16[256,8192]{1,0:T(8,128)(2,1)}, bf16[256,8192]{1,0:T(8,128)(2,1)S(1)}, u32[]{:S(2)}) copy-start(bf16[256,8192]{1,0:T(8,128)(2,1)S(1)} %fusion) | copy-start | bytes 12582916
  132.6 2.0 copy-start.2
  135.9 4.5 %copy-start = (f32[8192,256]{1,0:T(8,128)}, f32[8192,256]{1,0:T(8,128)S(1)}, u32[]{:S(2)}) copy-start(f32[8192,256]{1,0:T(8,128)S(1)} %convolution_add_fusion) | copy-start | bytes 25165828
  140.3 26.0 %collective-permute-start.1 = (f32[4096,256]{1,0:T(8,128)}, f32[4096,256]{1,0:T(8,128)}, u32[]{:S(2)}, u32[]{:S(2)}) collective-permute-start(f32[4096,256]{1,0:T(8,128)} %slice_select_fusion), channel_id=1, source_target_pairs={{0,4},{4,0},{8,12},{12,8},{1,5},{5,1},{9,13},{13,9},{2,6},{6,2},{1... | collective-permute-start | bytes 12582920 | tf_op jit(solution)/shard_map/ppermute | solution.py:14
  141.1 4.7 %copy-start.3 = (bf16[256,8192]{1,0:T(8,128)(2,1)S(1)}, bf16[256,8192]{1,0:T(8,128)(2,1)}, u32[]{:S(2)}) copy-start(bf16[256,8192]{1,0:T(8,128)(2,1)} %copy-done.2) | copy-start | bytes 12582916
  141.1 4.8 %copy-start.7 = (bf16[4096,256]{1,0:T(8,128)(2,1)S(1)}, bf16[4096,256]{1,0:T(8,128)(2,1)}, u32[]{:S(2)}) copy-start(bf16[4096,256]{1,0:T(8,128)(2,1)} %get-tuple-element.5) | copy-start | bytes 6291460
  147.7 0.8 copy-start.5
  148.5 111.6 %all-reduce.8.cloned.1.call-start = ((), (), s32[]{:S(2)}) async-start(), calls=%async_computation.7 | async-start | bytes 524288 | tf_op jit(solution)/shard_map/psum | solution.py:74
  151.7 142.7 %all-reduce.6.cloned.1.call-start = ((), (), s32[]{:S(2)}) async-start(), calls=%async_computation.6 | async-start | bytes 262144 | tf_op jit(solution)/shard_map/psum | solution.py:73
  166.3 207.5 %reduce-scatter.3.cloned.1.call-start = ((), (), s32[]{:S(2)}) async-start(), calls=%async_computation.4 | async-start | bytes 5242880 | tf_op jit(solution)/shard_map/reduce_scatter | solution.py:68
Sparse Core Ops, SparseCore 0:
  9.6 44.9 all-gather.1
  63.9 51.8 all-reduce.3
  148.6 17.6 reduce-scatter.4
  170.5 89.5 all-reduce.7
  262.3 32.0 all-reduce.5
  296.5 77.2 reduce-scatter.2
where the time goes:
time: 385 us; the launch traced here: 383 us
  waiting for transfers between devices  307 us (80%)
  matrix products  30 us (8%)
  other arithmetic  21 us (5%)
  between operations  14.3 us (4%)
  blocking collectives  6.31 us (2%)
    psum x1, waiting for transfers between devices, body(): core_total = lax.psum(acc_core, ('tile', 'cuts'))  78.2 us
    reduce_scatter x1, waiting for transfers between devices, body(): lax.psum_scatter(mine + received, 'cuts', scatter_dimension=0, tiled=True)  77.9 us
    psum x1, waiting for transfers between devices, from_root(): return lax.psum(block, axis)  52 us
    all_gather x1, waiting for transfers between devices, body(): own_block = lax.all_gather(factor, 'cuts', axis=0, tiled=True)  46.6 us
    psum x1, waiting for transfers between devices, body(): window_total = lax.psum(window_part, 'tile')  32.7 us
    reduce_scatter x1, waiting for transfers between devices, body(): lax.psum_scatter(padded, 'cuts', scatter_dimension=0, tiled=True)  14.5 us
    dot_general x2, matrix products, body(): lax.dot_general(mapped, column_factor, (((1,), (1,)), ((), ())), preferre...  13.9 us
  transfers between devices with their start and end apart: 8, of which 7 were waited for; matrix products, arithmetic and copies ran while one was open for 6% of the time, Pallas kernels for 0%

commit v1 on v0

v1 whole, which is shorter than its diff:
```python
import functools
import math

import jax
import jax.numpy as jnp
from jax import lax
from jax.experimental import pallas as pl
from jax.experimental.pallas import tpu as pltpu
from jax.sharding import PartitionSpec as P

HIGHEST = lax.Precision.HIGHEST
MESH = pl.DeviceIdType.MESH


def kernel(n, tiles, coef, trade, factor, scales, core, grad_ref, small_ref,
           tv, fac, win, acc, rbuf, fmat, bmat, bmat_t,
           tl_sem, ts_sem, tr_sem, own_sem, ag_send, ag_recv, rs_send, rs_recv, win_send, win_recv):
    z = lax.axis_index("cuts")
    t = lax.axis_index("tile")
    c = lax.rem(t, 2)
    partner = t + 1 - 2 * c
    months = trade.shape[0]
    rows = trade.shape[2]
    n_q, r = fac.shape[1], fac.shape[2]
    shard = n_q * r
    block = n * shard
    wsize = win.shape[0]
    pieces = win_recv.shape[0]
    wrow = wsize // pieces

    barrier = pltpu.get_barrier_semaphore()

    @pl.when(z > 0)
    def _():
        pl.semaphore_signal(barrier, inc=1, device_id={"cuts": z - 1}, device_id_type=MESH)

    @pl.when(z < n - 1)
    def _():
        pl.semaphore_signal(barrier, inc=1, device_id={"cuts": z + 1}, device_id_type=MESH)

    for k in range(1, tiles):
        pl.semaphore_signal(
            barrier, inc=1, device_id={"tile": lax.rem(t + k, tiles)}, device_id_type=MESH)

    def own_copy(q):
        return pltpu.make_async_copy(factor.at[pl.ds(q * r, r)], fac.at[z, q], own_sem.at[q])

    def local_trade(j, q):
        off = pl.multiple_of(c * block + j * shard + q * r, 128)
        return pltpu.make_async_copy(
            trade.at[:, 0, :, pl.ds(off, r)], tv.at[j, q, :, c], tl_sem.at[j, q])

    def remote_trade(j, q):
        off = pl.multiple_of((1 - c) * block + j * shard + q * r, 128)
        return pltpu.make_async_remote_copy(
            src_ref=trade.at[:, 0, :, pl.ds(off, r)], dst_ref=tv.at[j, q, :, c],
            send_sem=ts_sem.at[j, q], recv_sem=tr_sem.at[j, q],
            device_id={"tile": partner}, device_id_type=MESH)

    def recv_trade(j, q):
        off = pl.multiple_of(c * block + j * shard + q * r, 128)
        return pltpu.make_async_remote_copy(
            src_ref=trade.at[:, 0, :, pl.ds(off, r)], dst_ref=tv.at[j, q, :, 1 - c],
            send_sem=ts_sem.at[j, q], recv_sem=tr_sem.at[j, q],
            device_id={"tile": partner}, device_id_type=MESH)

    for q in range(n_q):
        own_copy(q).start()

    pl.semaphore_wait(
        barrier, tiles - 1 + jnp.where(z > 0, 1, 0) + jnp.where(z < n - 1, 1, 0))
    for q in range(n_q):
        own_copy(q).wait()

    def win_up(p):
        return pltpu.make_async_remote_copy(
            src_ref=win.at[pl.ds(p * wrow, wrow)], dst_ref=win.at[pl.ds(p * wrow, wrow)],
            send_sem=win_send.at[p, 0], recv_sem=win_recv.at[p],
            device_id={"cuts": z + 1}, device_id_type=MESH)

    def win_side(p, k):
        return pltpu.make_async_remote_copy(
            src_ref=win.at[pl.ds(p * wrow, wrow)], dst_ref=win.at[pl.ds(p * wrow, wrow)],
            send_sem=win_send.at[p, k], recv_sem=win_recv.at[p],
            device_id={"tile": k}, device_id_type=MESH)

    def win_recv_wait(p):
        win_up(p).wait_recv()

    @pl.when((t == 0) & (z == 0))
    def _():
        for p in range(pieces):
            win[pl.ds(p * wrow, wrow), :] = fac[0, p]

    @pl.when((t == 0) & (z == 0))
    def _():
        for p in range(pieces):
            if n > 1:
                win_up(p).start()
            for k in range(1, tiles):
                win_side(p, k).start()

    def mirrored(d, x):
        return jnp.where(d == 0, x, n - 1 - x)

    def ag_copy(d, j, q):
        return pltpu.make_async_remote_copy(
            src_ref=fac.at[j, q], dst_ref=fac.at[j, q],
            send_sem=ag_send.at[d, j, q], recv_sem=ag_recv.at[j, q],
            device_id={"cuts": z + 1 - 2 * d}, device_id_type=MESH)

    def gather_step(s, q):
        def one(d, carry):
            zm = mirrored(d, z)
            jm = zm - s

            @pl.when(jm >= 0)
            def _():
                j = mirrored(d, jm)

                @pl.when(s > 0)
                def _():
                    ag_copy(d, j, q).wait_recv()

                @pl.when(zm < n - 1)
                def _():
                    ag_copy(d, j, q).start()
            return carry
        lax.fori_loop(0, 2, one, 0)

    def gather_first(q, carry):
        gather_step(0, q)
        return carry
    lax.fori_loop(0, n_q, gather_first, 0)

    def trade_start(i, carry):
        s, q = i // n_q, i % n_q
        for d in (0, 1):
            zm = mirrored(d, z)

            @pl.when((zm - s >= 0) & ((s > 0) | (d == 0)))
            def _():
                j = mirrored(d, zm - s)
                local_trade(j, q).start()
                remote_trade(j, q).start()
        return carry
    lax.fori_loop(0, n * n_q, trade_start, 0)

    @pl.when((t != 0) | (z != 0))
    def _():
        for p in range(pieces):
            win_recv_wait(p)

            @pl.when(t == 0)
            def _():
                @pl.when(z < n - 1)
                def _():
                    win_up(p).start()
                for k in range(1, tiles):
                    win_side(p, k).start()

    def inner_of(m):
        drow = jnp.broadcast_to(scales[m:m + 1, :], core.shape)
        return drow.T * core[...] * drow

    win32 = win[...].astype(jnp.float32)
    for m in range(months):
        mapped = jnp.dot(win32, inner_of(m), precision=HIGHEST,
                         preferred_element_type=jnp.float32)
        bmat[m] = mapped.astype(jnp.bfloat16)
        bmat_t[m] = mapped.T.astype(jnp.bfloat16)
        fmat[m] = jnp.zeros_like(fmat[m])

    def compute(j, q):
        local_trade(j, q).wait()
        recv_trade(j, q).wait_recv()
        a = fac[j, q]
        total = None
        for m in range(months):
            x = jnp.concatenate([tv[j, q, m, 0], tv[j, q, m, 1]], 0)
            model = lax.dot_general(bmat[m], a, (((1,), (1,)), ((), ())),
                                    preferred_element_type=jnp.float32)
            e = (x.astype(jnp.float32) - model).astype(jnp.bfloat16)
            term = jnp.dot(bmat_t[m], e, preferred_element_type=jnp.float32)
            total = term if total is None else total + term
            fmat[m] += jnp.dot(e, a, preferred_element_type=jnp.float32)
        acc[j, q] = total

    def compute_step(s, q):
        def one(d, carry):
            jm = mirrored(d, z) - s

            @pl.when((jm >= 0) & ((s > 0) | (d == 0)))
            def _():
                compute(mirrored(d, jm), q)
            return carry
        lax.fori_loop(0, 2, one, 0)

    def rs_copy(d, j, q):
        to = z + 1 - 2 * d
        slot = jnp.where((j == to) & (d == 1), n, j)
        return pltpu.make_async_remote_copy(
            src_ref=acc.at[j, q], dst_ref=rbuf.at[slot, q],
            send_sem=rs_send.at[j, q], recv_sem=rs_recv.at[slot, q],
            device_id={"cuts": to}, device_id_type=MESH)

    def rs_wait(d, slot, q):
        pltpu.make_async_remote_copy(
            src_ref=acc.at[0, q], dst_ref=rbuf.at[slot, q],
            send_sem=rs_send.at[0, q], recv_sem=rs_recv.at[slot, q],
            device_id={"cuts": z + 1 - 2 * d}, device_id_type=MESH).wait_recv()

    def reduce_step(s, q):
        def one(d, carry):
            zm = mirrored(d, z)
            jm = s - zm

            @pl.when((jm > zm) & (jm <= n - 1))
            def _():
                j = mirrored(d, jm)

                @pl.when(zm > 0)
                def _():
                    rs_wait(d, j, q)
                    acc[j, q] = acc[j, q] + rbuf[j, q]
                rs_copy(d, j, q).start()
            return carry
        lax.fori_loop(0, 2, one, 0)

    def main_step(i, carry):
        s, q = i // n_q, i % n_q

        @pl.when(s > 0)
        def _():
            gather_step(s, q)
        compute_step(s, q)
        reduce_step(s, q)
        return carry
    lax.fori_loop(0, n * n_q, main_step, 0)

    win_t = win32.T
    window_sum = jnp.zeros((wsize, core.shape[1]), jnp.float32)
    core_sum = jnp.zeros(core.shape, jnp.float32)
    small_ref[pl.ds(wsize + core.shape[0], 8), :] = jnp.zeros((8, core.shape[1]), jnp.float32)
    for m in range(months):
        drow = jnp.broadcast_to(scales[m:m + 1, :], core.shape)
        dcol = drow.T
        inner = dcol * core[...] * drow
        window_sum += lax.dot_general(fmat[m], inner, (((1,), (1,)), ((), ())),
                                      precision=HIGHEST, preferred_element_type=jnp.float32)
        gram = jnp.dot(win_t, fmat[m], precision=HIGHEST, preferred_element_type=jnp.float32)
        core_sum += dcol * gram * drow
        weighted = gram * core[...]
        by_row = jnp.sum(weighted.T * dcol, axis=0, keepdims=True)
        by_col = jnp.sum(weighted * dcol, axis=0, keepdims=True)
        small_ref[pl.ds(wsize + core.shape[0] + m, 1), :] = -coef * (by_row + by_col)
    small_ref[pl.ds(0, wsize), :] = -coef * window_sum
    small_ref[pl.ds(wsize, core.shape[0]), :] = -coef * core_sum

    def tail_step(i, carry):
        reduce_step(i // n_q, i % n_q)
        return carry
    lax.fori_loop(n * n_q, (2 * n - 1) * n_q, tail_step, 0)

    for q in range(n_q):
        @pl.when(z > 0)
        def _():
            rs_wait(0, z, q)
            acc[z, q] = acc[z, q] + rbuf[z, q]

        @pl.when(z < n - 1)
        def _():
            rs_wait(1, n, q)
            acc[z, q] = acc[z, q] + rbuf[n, q]
        grad_ref[pl.ds(q * r, r), :] = -coef * acc[z, q].T

    def drain(i, carry):
        j, q = i // n_q, i % n_q
        remote_trade(j, q).wait_send()

        @pl.when((j <= z) & (z < n - 1))
        def _():
            ag_copy(0, j, q).wait_send()

        @pl.when((j >= z) & (z > 0))
        def _():
            ag_copy(1, j, q).wait_send()

        @pl.when(j != z)
        def _():
            rs_copy(jnp.where(j > z, 0, 1), j, q).wait_send()
        return carry
    lax.fori_loop(0, n * n_q, drain, 0)

    @pl.when(t == 0)
    def _():
        for p in range(pieces):
            @pl.when(z < n - 1)
            def _():
                win_up(p).wait_send()
            for k in range(1, tiles):
                win_side(p, k).wait_send()


def fused(n, tiles, trade, factor, scales, core):
    months, rows, size = trade.shape[0], trade.shape[2], factor.shape[1]
    shard = factor.shape[0]
    r = 256
    n_q = shard // r
    wsize = 2 * rows
    pieces = wsize // r
    coef = 1.0 / math.sqrt(months * n * wsize)
    vmem = pl.BlockSpec(memory_space=pltpu.VMEM)
    anyspace = pl.BlockSpec(memory_space=pl.ANY)
    dma = pltpu.SemaphoreType.DMA
    return pl.pallas_call(
        functools.partial(kernel, n, tiles, coef),
        out_shape=(jax.ShapeDtypeStruct((shard, size), jnp.float32),
                   jax.ShapeDtypeStruct((wsize + size + 8, size), jnp.float32)),
        in_specs=[anyspace, anyspace, vmem, vmem],
        out_specs=(vmem, vmem),
        scratch_shapes=[
            pltpu.VMEM((n, n_q, months, 2, rows, r), jnp.bfloat16),
            pltpu.VMEM((n, n_q, r, size), jnp.bfloat16),
            pltpu.VMEM((wsize, size), jnp.bfloat16),
            pltpu.VMEM((n, n_q, size, r), jnp.float32),
            pltpu.VMEM((n + 1, n_q, size, r), jnp.float32),
            pltpu.VMEM((months, wsize, size), jnp.float32),
            pltpu.VMEM((months, wsize, size), jnp.bfloat16),
            pltpu.VMEM((months, size, wsize), jnp.bfloat16),
            dma((n, n_q)), dma((n, n_q)), dma((n, n_q)), dma((n_q,)),
            dma((2, n, n_q)), dma((n, n_q)), dma((n, n_q)), dma((n + 1, n_q)),
            dma((pieces, tiles)), dma((pieces,)),
        ],
        compiler_params=pltpu.CompilerParams(
            collective_id=0, has_side_effects=True, vmem_limit_bytes=56 * 2**20),
    )(trade, factor, scales, core)


def small_sums(n, small, wsize, size, months):
    z = lax.axis_index("cuts")
    diag = jnp.zeros((months * n, size), jnp.float32)
    diag = lax.dynamic_update_slice_in_dim(
        diag, small[wsize + size:wsize + size + months], z * months, 0)
    total = lax.psum(jnp.concatenate([small[:wsize + size], diag], 0), ("tile", "cuts"))
    window = lax.dynamic_slice_in_dim(total, z * (wsize // n), wsize // n, 0)
    diag = lax.dynamic_slice_in_dim(total, wsize + size + z * months, months, 0)
    return window, total[wsize:wsize + size], diag


def swapped(value, axis, distance):
    mask = 2**distance
    pairs = [(source, source ^ mask) for source in range(lax.axis_size(axis))]
    return lax.ppermute(value, axis, pairs)


def plain(trade, factor, scales, core):
    n = lax.axis_size("cuts")
    band_index = lax.axis_index("tile") % 2
    months, rows, size = trade.shape[0], trade.shape[2], factor.shape[1]
    wsize = 2 * rows
    own = lax.all_gather(factor, "cuts", axis=0, tiled=True)
    block = own.shape[0]
    partner = swapped(own, "tile", 0)
    columns = jnp.concatenate([jnp.where(band_index == 0, own, partner),
                               jnp.where(band_index == 0, partner, own)], 0)
    first = jnp.where(lax.axis_index("tile") == 0, own[:wsize], jnp.zeros_like(own[:wsize]))
    window = lax.psum(first, "tile")
    window32 = lax.dynamic_slice_in_dim(window, band_index * rows, rows, 0).astype(jnp.float32)
    coef = 1.0 / math.sqrt(months * n * wsize)
    acc_columns = jnp.zeros((2 * block, size), jnp.float32)
    acc_window = jnp.zeros((rows, size), jnp.float32)
    acc_core = jnp.zeros((size, size), jnp.float32)
    diags = []
    for month in range(months):
        diag_k = scales[month]
        inner = diag_k[:, None] * core * diag_k[None, :]
        mapped = jnp.dot(window32, inner, precision=HIGHEST).astype(jnp.bfloat16)
        model = lax.dot_general(mapped, columns, (((1,), (1,)), ((), ())),
                                preferred_element_type=jnp.float32)
        residual = (trade[month, 0].astype(jnp.float32) - model).astype(jnp.bfloat16)
        acc_columns = acc_columns + lax.dot_general(
            residual, mapped, (((0,), (0,)), ((), ())), preferred_element_type=jnp.float32)
        projected = jnp.dot(residual, columns, preferred_element_type=jnp.float32)
        acc_window = acc_window + jnp.dot(projected, inner.T, precision=HIGHEST)
        gram = jnp.dot(window32.T, projected, precision=HIGHEST)
        acc_core = acc_core + diag_k[:, None] * gram * diag_k[None, :]
        weighted = gram * core
        diags.append(jnp.dot(weighted, diag_k, precision=HIGHEST)
                     + jnp.dot(weighted.T, diag_k, precision=HIGHEST))
    halves = acc_columns.reshape(2, block, size)
    mine = jnp.where(band_index == 0, halves[0], halves[1])
    other = jnp.where(band_index == 0, halves[1], halves[0])
    grad = lax.psum_scatter(mine + swapped(other, "tile", 0), "cuts",
                            scatter_dimension=0, tiled=True)
    padded = lax.dynamic_update_slice_in_dim(
        jnp.zeros((wsize, size), jnp.float32), acc_window, band_index * rows, 0)
    small = jnp.concatenate([padded, acc_core, jnp.stack(diags, 0)], 0)
    window, core_total, diag = small_sums(n, -coef * small, wsize, size, months)
    return -coef * grad, window, core_total, diag


def body(trade, factor, scales, core):
    n, tiles = lax.axis_size("cuts"), lax.axis_size("tile")
    months, wsize, size = trade.shape[0], 2 * trade.shape[2], factor.shape[1]
    if factor.shape[0] % 256 or factor.shape[0] < wsize or n < 2:
        return plain(trade, factor, scales, core)
    grad, small = fused(n, tiles, trade, factor, scales, core)
    window, core_total, diag = small_sums(n, small, wsize, size, months)
    return grad, window, core_total, diag


def solution(mesh):
    return jax.shard_map(
        body,
        mesh=mesh,
        in_specs=(
            P(("groups", "cuts"), "tile", None, None),
            P(("groups", "tile", "cuts"), None),
            P(("groups", "cuts"), None),
            P("groups", None),
        ),
        out_specs=(
            P(("groups", "tile", "cuts"), None),
            P(("groups", "cuts"), None),
            P("groups", None),
            P(("groups", "cuts"), None),
        ),
        check_vma=False,
    )
```

time: 385 us -> 248 us (0.64)
  waiting for transfers between devices: 307 us -> 96.2 us
  Pallas kernels: 0 us -> 125 us
  matrix products: 30 us -> 0 us
  other arithmetic: 21 us -> 0.94 us
  blocking collectives: 6.31 us -> 0 us
  local copies, waits for them, and re-layouts: 3.15 us -> 8.67 us
    pallas_call x0 -> x1, Pallas kernels: none -> 125 us  [fused(): pl.pallas_call(functools.partial(kernel, n, tiles, coef), out_shape=(jax....]
    reduce_scatter x2 -> x0, waiting for transfers between devices: 92.4 us -> none  [the longest x1 77.9 us: body(): lax.psum_scatter(mine + received, 'cuts', scatter_dimension=0, tiled=True)]
    psum x3 -> x1, waiting for transfers between devices: 163 us -> 96.2 us  [small_sums(): lax.psum(jnp.concatenate([small[:wsize + size], diag], 0), ('tile', 'cuts'))]
    all_gather x1 -> x0, waiting for transfers between devices: 46.6 us -> none  [body(): own_block = lax.all_gather(factor, 'cuts', axis=0, tiled=True)]
    dot_general x16 -> x0, matrix products: 30 us -> none  [the longest x2 13.9 us: body(): lax.dot_general(mapped, column_factor, (((1,), (1,)), ((), ())), preferre...]
    select_n x2 -> x0, other arithmetic: 7.45 us -> none  [the longest x1 4.63 us: body(): first_block = jnp.where(band_index == 0, own_block, partner_block)]
    add x3 -> x0, other arithmetic: 7.41 us -> none  [the longest x1 7.4 us: body(): mine + received]
    psum x1 -> x0, blocking collectives: 6.31 us -> none  [body(): diag_total = lax.psum(diag_stack, 'tile')]
  transfers between devices with their start and end apart: 8 -> 1, of which waited for: 7 -> 1; matrix products, arithmetic and copies ran while one was open for 6% -> 0% of each run, Pallas kernels for 0% -> 0%
where the time goes in v1:
time: 248 us; the launch traced here: 245 us
  Pallas kernels  125 us (50%)
  waiting for transfers between devices  96.2 us (39%)
  between operations  14.1 us (6%)
  local copies, waits for them, and re-layouts  8.67 us (3%)
    pallas_call x1, Pallas kernels, fused(): pl.pallas_call(functools.partial(kernel, n, tiles, coef), out_shape=(jax....  125 us
    psum x1, waiting for transfers between devices, small_sums(): lax.psum(jnp.concatenate([small[:wsize + size], diag], 0), ('tile', 'cuts'))  96.2 us
  transfers between devices with their start and end apart: 1, of which 1 were waited for; matrix products, arithmetic and copies ran while one was open for 0% of the time, Pallas kernels for 0%

profile of v1, /device:TPU:25, one launch (start us, length us, event | category | flops | bytes accessed | tf_op | source)
XLA Modules:
  0.0 244.7 jit_solution(5127807774744798485)
XLA Ops:
  7.2 0.0 all-reduce.2.cloned.1.call-start
  7.2 124.7 %shard_map.75 = (f32[1024,256]{1,0:T(8,128)}, f32[776,256]{1,0:T(8,128)}) custom-call(bf16[2,1,256,8192]{3,2,1,0:T(8,128)(2,1)} %trade.1, bf16[1024,256]{1,0:T(8,128)(2,1)} %factor.1, f32[2,256]{1,0:T(2,128)} %scales.1, f32[256,256]{1,0:T(8,128)} %core.1), custom_call_target="tpu_custom_call" | custom-call | tf_op jit(solution)/shard_map/pallas_call | solution.py:316
  131.9 1.2 slice.9
  133.1 0.7 slice_dynamic-update-slice_fusion
  133.9 0.9 pad_maximum_fusion
  134.8 0.0 all-reduce.2.cloned.1.call-update
  134.8 96.2 %all-reduce.2.cloned.1.call-done = f32[776,256]{1,0:T(8,128)} async-done(((f32[776,256]{1,0:T(8,128)}), f32[776,256]{1,0:T(8,128)}) %all-reduce.2.cloned.1.call-update) | async-done | bytes 794640 | tf_op jit(solution)/shard_map/psum | solution.py:345
  231.0 1.7 slice.12
  232.7 1.3 constant_dynamic-slice_fusion
  234.0 1.6 constant_dynamic-slice_fusion.1
  235.5 2.3 copy.11
  (1 shorter events, 0.0 us)
Async XLA Ops:
  7.2 223.9 %all-reduce.2.cloned.1.call-start = ((), (), s32[]{:S(2)}) async-start(), calls=%async_computation | async-start | bytes 1589248 | tf_op jit(solution)/shard_map/psum | solution.py:345
Sparse Core Ops, SparseCore 0:
  134.9 96.0 all-reduce.1

commit v2 on v1

--- a/solution.py
+++ b/solution.py
@@ -12,9 +12,12 @@
 MESH = pl.DeviceIdType.MESH
 
 
-def kernel(n, tiles, coef, trade, factor, scales, core, grad_ref, small_ref,
+def kernel(n, tiles, coef, trade, factor, scales, core, grad_ref, wout_ref, core_ref, diag_ref,
            tv, fac, win, acc, rbuf, fmat, bmat, bmat_t,
-           tl_sem, ts_sem, tr_sem, own_sem, ag_send, ag_recv, rs_send, rs_recv, win_send, win_recv):
+           part, p1buf, s2, p2buf, cfin, wfin, dbuf,
+           tl_sem, ts_sem, tr_sem, own_sem, ag_send, ag_recv, rs_send, rs_recv, win_send, win_recv,
+           p1_send, p1_recv, p2_send, p2_recv, p3_send, p3_recv, p4_send, p4_recv, p5_send, p5_recv,
+           d_send, d_recv):
     z = lax.axis_index("cuts")
     t = lax.axis_index("tile")
     c = lax.rem(t, 2)
@@ -30,14 +33,9 @@
 
     barrier = pltpu.get_barrier_semaphore()
 
-    @pl.when(z > 0)
-    def _():
-        pl.semaphore_signal(barrier, inc=1, device_id={"cuts": z - 1}, device_id_type=MESH)
-
-    @pl.when(z < n - 1)
-    def _():
-        pl.semaphore_signal(barrier, inc=1, device_id={"cuts": z + 1}, device_id_type=MESH)
-
+    for k in range(1, n):
+        pl.semaphore_signal(
+            barrier, inc=1, device_id={"cuts": lax.rem(z + k, n)}, device_id_type=MESH)
     for k in range(1, tiles):
         pl.semaphore_signal(
             barrier, inc=1, device_id={"tile": lax.rem(t + k, tiles)}, device_id_type=MESH)
@@ -67,8 +65,7 @@
     for q in range(n_q):
         own_copy(q).start()
 
-    pl.semaphore_wait(
-        barrier, tiles - 1 + jnp.where(z > 0, 1, 0) + jnp.where(z < n - 1, 1, 0))
+    pl.semaphore_wait(barrier, tiles + n - 2)
     for q in range(n_q):
         own_copy(q).wait()
 
@@ -241,7 +238,7 @@
     win_t = win32.T
     window_sum = jnp.zeros((wsize, core.shape[1]), jnp.float32)
     core_sum = jnp.zeros(core.shape, jnp.float32)
-    small_ref[pl.ds(wsize + core.shape[0], 8), :] = jnp.zeros((8, core.shape[1]), jnp.float32)
+    diags = []
     for m in range(months):
         drow = jnp.broadcast_to(scales[m:m + 1, :], core.shape)
         dcol = drow.T
@@ -253,14 +250,116 @@
         weighted = gram * core[...]
         by_row = jnp.sum(weighted.T * dcol, axis=0, keepdims=True)
         by_col = jnp.sum(weighted * dcol, axis=0, keepdims=True)
-        small_ref[pl.ds(wsize + core.shape[0] + m, 1), :] = -coef * (by_row + by_col)
-    small_ref[pl.ds(0, wsize), :] = -coef * window_sum
-    small_ref[pl.ds(wsize, core.shape[0]), :] = -coef * core_sum
+        diags.append(-coef * (by_row + by_col))
+    wr, cr = wfin.shape[1], cfin.shape[2]
+    for k in range(tiles):
+        for i in range(n):
+            w0, c0 = (i * tiles + k) * wr, (i * tiles + k) * cr
+            part[k, i, pl.ds(0, wr), :] = -coef * window_sum[w0:w0 + wr]
+            part[k, i, pl.ds(wr, cr), :] = -coef * core_sum[c0:c0 + cr]
+    dbuf[t] = jnp.concatenate(
+        diags + [jnp.zeros((8 - months, core.shape[1]), jnp.float32)], 0)
+
+    def peer_t(k):
+        return lax.rem(t + k, tiles)
+
+    def peer_z(k):
+        return lax.rem(z + k, n)
+
+    def to_tile(src, dst, send, recv, k, who):
+        return pltpu.make_async_remote_copy(
+            src_ref=src, dst_ref=dst, send_sem=send.at[k], recv_sem=recv.at[who],
+            device_id={"tile": peer_t(k)}, device_id_type=MESH)
+
+    def to_cut(src, dst, send, recv, k, who):
+        return pltpu.make_async_remote_copy(
+            src_ref=src, dst_ref=dst, send_sem=send.at[k], recv_sem=recv.at[who],
+            device_id={"cuts": peer_z(k)}, device_id_type=MESH)
+
+    def p1(k, who):
+        return to_tile(part.at[peer_t(k)], p1buf.at[who], p1_send, p1_recv, k, who)
+
+    def pd(k, who):
+        return to_tile(dbuf.at[who], dbuf.at[who], d_send, d_recv, k, who)
+
+    def p2(k, who):
+        return to_cut(s2.at[peer_z(k)], p2buf.at[who], p2_send, p2_recv, k, who)
+
+    def p3(k, who):
+        return to_cut(cfin.at[who, t], cfin.at[who, t], p3_send, p3_recv, k, who)
+
+    def p4(k, who):
+        return to_tile(cfin.at[:, who], cfin.at[:, who], p4_send, p4_recv, k, who)
+
+    def p5(k, who):
+        return to_tile(wfin.at[who], wfin.at[who], p5_send, p5_recv, k, who)
+
+    for k in range(1, tiles):
+        p1(k, t).start()
+        pd(k, t).start()
+
+    def small_second():
+        for k in range(1, tiles):
+            p1(k, peer_t(k)).wait_recv()
+        total = part[t]
+        for k in range(1, tiles):
+            total = total + p1buf[peer_t(k)]
+        s2[...] = total
+        for k in range(1, n):
+            p2(k, z).start()
+
+    def small_third():
+        for k in range(1, n):
+            p2(k, peer_z(k)).wait_recv()
+        total = s2[z]
+        for k in range(1, n):
+            total = total + p2buf[peer_z(k)]
+        wfin[t] = total[:wr]
+        cfin[z, t] = total[wr:]
+        for k in range(1, n):
+            p3(k, z).start()
+        for k in range(1, tiles):
+            p5(k, t).start()
+
+    def small_fourth():
+        for k in range(1, n):
+            p3(k, peer_z(k)).wait_recv()
+        for k in range(1, tiles):
+            p4(k, t).start()
+
+    def small_last():
+        for k in range(1, tiles):
+            p4(k, peer_t(k)).wait_recv()
+            p5(k, peer_t(k)).wait_recv()
+            pd(k, peer_t(k)).wait_recv()
+        for k in range(tiles):
+            wout_ref[pl.ds(k * wr, wr), :] = wfin[k]
+            for i in range(n):
+                core_ref[pl.ds((i * tiles + k) * cr, cr), :] = cfin[i, k]
+        total = dbuf[0]
+        for k in range(1, tiles):
+            total = total + dbuf[k]
+        diag_ref[...] = total[:months]
+        for k in range(1, tiles):
+            p1(k, t).wait_send()
+            pd(k, t).wait_send()
+            p4(k, t).wait_send()
+            p5(k, t).wait_send()
+        for k in range(1, n):
+            p2(k, z).wait_send()
+            p3(k, z).wait_send()
 
     def tail_step(i, carry):
         reduce_step(i // n_q, i % n_q)
         return carry
-    lax.fori_loop(n * n_q, (2 * n - 1) * n_q, tail_step, 0)
+
+    stages = [small_second, small_third, small_fourth]
+    for s in range(n, 2 * n - 1):
+        lax.fori_loop(s * n_q, (s + 1) * n_q, tail_step, 0)
+        if stages:
+            stages.pop(0)()
+    for stage in stages:
+        stage()
 
     for q in range(n_q):
         @pl.when(z > 0)
@@ -273,6 +372,8 @@
             rs_wait(1, n, q)
             acc[z, q] = acc[z, q] + rbuf[n, q]
         grad_ref[pl.ds(q * r, r), :] = -coef * acc[z, q].T
+
+    small_last()
 
     def drain(i, carry):
         j, q = i // n_q, i % n_q
@@ -309,6 +410,7 @@
     n_q = shard // r
     wsize = 2 * rows
     pieces = wsize // r
+    wr, cr = wsize // (n * tiles), size // (n * tiles)
     coef = 1.0 / math.sqrt(months * n * wsize)
     vmem = pl.BlockSpec(memory_space=pltpu.VMEM)
     anyspace = pl.BlockSpec(memory_space=pl.ANY)
@@ -316,9 +418,11 @@
     return pl.pallas_call(
         functools.partial(kernel, n, tiles, coef),
         out_shape=(jax.ShapeDtypeStruct((shard, size), jnp.float32),
-                   jax.ShapeDtypeStruct((wsize + size + 8, size), jnp.float32)),
+                   jax.ShapeDtypeStruct((wsize // n, size), jnp.float32),
+                   jax.ShapeDtypeStruct((size, size), jnp.float32),
+                   jax.ShapeDtypeStruct((months, size), jnp.float32)),
         in_specs=[anyspace, anyspace, vmem, vmem],
-        out_specs=(vmem, vmem),
+        out_specs=(vmem, vmem, vmem, vmem),
         scratch_shapes=[
             pltpu.VMEM((n, n_q, months, 2, rows, r), jnp.bfloat16),
             pltpu.VMEM((n, n_q, r, size), jnp.bfloat16),
@@ -328,9 +432,18 @@
             pltpu.VMEM((months, wsize, size), jnp.float32),
             pltpu.VMEM((months, wsize, size), jnp.bfloat16),
             pltpu.VMEM((months, size, wsize), jnp.bfloat16),
+            pltpu.VMEM((tiles, n, wr + cr, size), jnp.float32),
+            pltpu.VMEM((tiles, n, wr + cr, size), jnp.float32),
+            pltpu.VMEM((n, wr + cr, size), jnp.float32),
+            pltpu.VMEM((n, wr + cr, size), jnp.float32),
+            pltpu.VMEM((n, tiles, cr, size), jnp.float32),
+            pltpu.VMEM((tiles, wr, size), jnp.float32),
+            pltpu.VMEM((tiles, 8, size), jnp.float32),
             dma((n, n_q)), dma((n, n_q)), dma((n, n_q)), dma((n_q,)),
             dma((2, n, n_q)), dma((n, n_q)), dma((n, n_q)), dma((n + 1, n_q)),
             dma((pieces, tiles)), dma((pieces,)),
+            dma((tiles,)), dma((tiles,)), dma((n,)), dma((n,)), dma((n,)), dma((n,)),
+            dma((tiles,)), dma((tiles,)), dma((tiles,)), dma((tiles,)), dma((tiles,)), dma((tiles,)),
         ],
         compiler_params=pltpu.CompilerParams(
             collective_id=0, has_side_effects=True, vmem_limit_bytes=56 * 2**20),
@@ -403,11 +516,11 @@
 def body(trade, factor, scales, core):
     n, tiles = lax.axis_size("cuts"), lax.axis_size("tile")
     months, wsize, size = trade.shape[0], 2 * trade.shape[2], factor.shape[1]
-    if factor.shape[0] % 256 or factor.shape[0] < wsize or n < 2:
+    if factor.shape[0] % 256 or factor.shape[0] < wsize or n < 2 or months > 8:
         return plain(trade, factor, scales, core)
-    grad, small = fused(n, tiles, trade, factor, scales, core)
-    window, core_total, diag = small_sums(n, small, wsize, size, months)
-    return grad, window, core_total, diag
+    if wsize % (8 * n * tiles) or size % (8 * n * tiles):
+        return plain(trade, factor, scales, core)
+    return fused(n, tiles, trade, factor, scales, core)
 
 
 def solution(mesh):

time: 248 us -> 145 us (0.58); the launches traced: 245 us -> 145 us
  waiting for transfers between devices: 96.2 us -> 0 us
  between operations: 14.1 us -> 0.64 us
  Pallas kernels: 125 us -> 138 us
    psum x1 -> x0, waiting for transfers between devices: 96.2 us -> none  [small_sums(): lax.psum(jnp.concatenate([small[:wsize + size], diag], 0), ('tile', 'cuts'))]
    pallas_call x1, Pallas kernels: 125 us -> 138 us  [fused(): pl.pallas_call(functools.partial(kernel, n, tiles, coef), out_shape=(jax....]
    unnamed x1 -> x4, local copies, waits for them, and re-layouts: 2.26 us -> 6.74 us
    slice x2 -> x0, local copies, waits for them, and re-layouts: 2.85 us -> none  [the longest x1 1.67 us: small_sums(): return (window, total[wsize:wsize + size], diag)]
    dynamic_slice x2 -> x0, local copies, waits for them, and re-layouts: 2.84 us -> none  [the longest x1 1.57 us: small_sums(): window = lax.dynamic_slice_in_dim(total, z * (wsize // n), wsize // n, 0)]
  transfers between devices with their start and end apart: 1 -> 0, of which waited for: 1 -> 0; matrix products, arithmetic and copies ran while one was open for 0% -> 0% of each run, Pallas kernels for 0% -> 0%
where the time goes in v2:
time: 145 us
  Pallas kernels  138 us (95%)
  local copies, waits for them, and re-layouts  6.74 us (5%)
    pallas_call x1, Pallas kernels, fused(): pl.pallas_call(functools.partial(kernel, n, tiles, coef), out_shape=(jax....  138 us
    unnamed x4, local copies, waits for them, and re-layouts  6.74 us

profile of v2, /device:TPU:25, one launch (start us, length us, event | category | flops | bytes accessed | tf_op | source)
XLA Modules:
  0.0 145.1 jit_solution(309134646886700276)
XLA Ops:
  0.6 137.7 %shard_map.75 = (f32[1024,256]{1,0:T(8,128)}, f32[128,256]{1,0:T(8,128)}, f32[256,256]{1,0:T(8,128)}, f32[2,256]{1,0:T(2,128)}) custom-call(bf16[2,1,256,8192]{3,2,1,0:T(8,128)(2,1)} %trade.1, bf16[1024,256]{1,0:T(8,128)(2,1)} %factor.1, f32[2,256]{1,0:T(2,128)} %scales.1, f32[256,256]{1,0:T(8,128)} %core.1), custom_call_target="tpu_custom_call" | custom-call | tf_op jit(solution)/shard_map/pallas_call | solution.py:418
  138.4 2.3 %copy.12 = f32[1024,256]{1,0:T(8,128)} copy(f32[1024,256]{1,0:T(8,128)} %get-tuple-element.8) | data formatting | bytes 2097152
  140.6 1.6 %copy.13 = f32[128,256]{1,0:T(8,128)} copy(f32[128,256]{1,0:T(8,128)} %get-tuple-element.9) | data formatting | bytes 262144
  142.2 1.7 %copy.14 = f32[256,256]{1,0:T(8,128)} copy(f32[256,256]{1,0:T(8,128)} %get-tuple-element.10) | data formatting | bytes 524288
  143.9 1.2 copy.15

commit v3 on v2

--- a/solution.py
+++ b/solution.py
@@ -12,8 +12,29 @@
 MESH = pl.DeviceIdType.MESH
 
 
+SPAN = 250.0
+
+
+def encode(ref, x):
+    size = x.shape[0]
+    top = jnp.maximum(jnp.max(jnp.abs(x), axis=0, keepdims=True), 1e-30)
+    scale = (top * 1.008).astype(jnp.bfloat16).astype(jnp.float32)
+    u = x * (1.0 / scale)
+    a = jnp.exp2(jnp.abs(u) * SPAN - 0.5 * SPAN)
+    ref[pl.ds(0, size), :] = jnp.where(u < 0.0, -a, a).astype(jnp.bfloat16)
+    ref[pl.ds(size, 16), :] = jnp.broadcast_to(scale, (16, x.shape[1])).astype(jnp.bfloat16)
+
+
+def decode(ref):
+    size = ref.shape[0] - 16
+    y = ref[pl.ds(0, size), :].astype(jnp.float32)
+    scale = ref[pl.ds(size, 16), :].astype(jnp.float32)[:1]
+    u = jnp.log(jnp.abs(y)) * (1.0 / (SPAN * math.log(2.0))) + 0.5
+    return jnp.where(y < 0.0, -u, u) * scale
+
+
 def kernel(n, tiles, coef, trade, factor, scales, core, grad_ref, wout_ref, core_ref, diag_ref,
-           tv, fac, win, acc, rbuf, fmat, bmat, bmat_t,
+           tv, fac, win, acc, sbuf, rbuf, fmat, bmat, bmat_t,
            part, p1buf, s2, p2buf, cfin, wfin, dbuf,
            tl_sem, ts_sem, tr_sem, own_sem, ag_send, ag_recv, rs_send, rs_recv, win_send, win_recv,
            p1_send, p1_recv, p2_send, p2_recv, p3_send, p3_recv, p4_send, p4_recv, p5_send, p5_recv,
@@ -197,13 +218,13 @@
         to = z + 1 - 2 * d
         slot = jnp.where((j == to) & (d == 1), n, j)
         return pltpu.make_async_remote_copy(
-            src_ref=acc.at[j, q], dst_ref=rbuf.at[slot, q],
+            src_ref=sbuf.at[j, q], dst_ref=rbuf.at[slot, q],
             send_sem=rs_send.at[j, q], recv_sem=rs_recv.at[slot, q],
             device_id={"cuts": to}, device_id_type=MESH)
 
     def rs_wait(d, slot, q):
         pltpu.make_async_remote_copy(
-            src_ref=acc.at[0, q], dst_ref=rbuf.at[slot, q],
+            src_ref=sbuf.at[0, q], dst_ref=rbuf.at[slot, q],
             send_sem=rs_send.at[0, q], recv_sem=rs_recv.at[slot, q],
             device_id={"cuts": z + 1 - 2 * d}, device_id_type=MESH).wait_recv()
 
@@ -219,7 +240,8 @@
                 @pl.when(zm > 0)
                 def _():
                     rs_wait(d, j, q)
-                    acc[j, q] = acc[j, q] + rbuf[j, q]
+                    acc[j, q] = acc[j, q] + decode(rbuf.at[j, q])
+                encode(sbuf.at[j, q], acc[j, q])
                 rs_copy(d, j, q).start()
             return carry
         lax.fori_loop(0, 2, one, 0)
@@ -365,12 +387,12 @@
         @pl.when(z > 0)
         def _():
             rs_wait(0, z, q)
-            acc[z, q] = acc[z, q] + rbuf[z, q]
+            acc[z, q] = acc[z, q] + decode(rbuf.at[z, q])
 
         @pl.when(z < n - 1)
         def _():
             rs_wait(1, n, q)
-            acc[z, q] = acc[z, q] + rbuf[n, q]
+            acc[z, q] = acc[z, q] + decode(rbuf.at[n, q])
         grad_ref[pl.ds(q * r, r), :] = -coef * acc[z, q].T
 
     small_last()
@@ -428,7 +450,8 @@
             pltpu.VMEM((n, n_q, r, size), jnp.bfloat16),
             pltpu.VMEM((wsize, size), jnp.bfloat16),
             pltpu.VMEM((n, n_q, size, r), jnp.float32),
-            pltpu.VMEM((n + 1, n_q, size, r), jnp.float32),
+            pltpu.VMEM((n, n_q, size + 16, r), jnp.bfloat16),
+            pltpu.VMEM((n + 1, n_q, size + 16, r), jnp.bfloat16),
             pltpu.VMEM((months, wsize, size), jnp.float32),
             pltpu.VMEM((months, wsize, size), jnp.bfloat16),
             pltpu.VMEM((months, size, wsize), jnp.bfloat16),

time: 145 us -> 105 us (0.72); the launches traced: 145 us -> 103 us
  Pallas kernels: 138 us -> 96.1 us
    pallas_call x1, Pallas kernels: 138 us -> 96.1 us  [fused(): pl.pallas_call(functools.partial(kernel, n, tiles, coef), out_shape=(jax....]
where the time goes in v3:
time: 105 us; the launch traced here: 103 us
  Pallas kernels  96.1 us (92%)
  local copies, waits for them, and re-layouts  6.74 us (6%)
    pallas_call x1, Pallas kernels, fused(): pl.pallas_call(functools.partial(kernel, n, tiles, coef), out_shape=(jax....  96.1 us
    unnamed x4, local copies, waits for them, and re-layouts  6.74 us

profile of v3, /device:TPU:25, one launch (start us, length us, event | category | flops | bytes accessed | tf_op | source)
XLA Modules:
  0.0 103.5 jit_solution(9404612986402500879)
XLA Ops:
  0.6 96.1 %shard_map.75 = (f32[1024,256]{1,0:T(8,128)}, f32[128,256]{1,0:T(8,128)}, f32[256,256]{1,0:T(8,128)}, f32[2,256]{1,0:T(2,128)}) custom-call(bf16[2,1,256,8192]{3,2,1,0:T(8,128)(2,1)} %trade.1, bf16[1024,256]{1,0:T(8,128)(2,1)} %factor.1, f32[2,256]{1,0:T(2,128)} %scales.1, f32[256,256]{1,0:T(8,128)} %core.1), custom_call_target="tpu_custom_call" | custom-call | tf_op jit(solution)/shard_map/pallas_call | solution.py:440
  96.7 2.3 %copy.12 = f32[1024,256]{1,0:T(8,128)} copy(f32[1024,256]{1,0:T(8,128)} %get-tuple-element.8) | data formatting | bytes 2097152
  99.0 1.6 %copy.13 = f32[128,256]{1,0:T(8,128)} copy(f32[128,256]{1,0:T(8,128)} %get-tuple-element.9) | data formatting | bytes 262144
  100.5 1.7 %copy.14 = f32[256,256]{1,0:T(8,128)} copy(f32[256,256]{1,0:T(8,128)} %get-tuple-element.10) | data formatting | bytes 524288
  102.2 1.2 %copy.15 = f32[2,256]{1,0:T(2,128)} copy(f32[2,256]{1,0:T(2,128)} %get-tuple-element.11) | data formatting | bytes 4096

commit v4 on v3

--- a/solution.py
+++ b/solution.py
@@ -113,8 +113,7 @@
     @pl.when((t == 0) & (z == 0))
     def _():
         for p in range(pieces):
-            if n > 1:
-                win_up(p).start()
+            win_up(p).start()
             for k in range(1, tiles):
                 win_side(p, k).start()
 
@@ -146,10 +145,15 @@
             return carry
         lax.fori_loop(0, 2, one, 0)
 
-    def gather_first(q, carry):
-        gather_step(0, q)
-        return carry
-    lax.fori_loop(0, n_q, gather_first, 0)
+    early = jnp.where(t >= 2, n_q, jnp.where(z > 0, n_q // 2, 0))
+    for q in range(n_q):
+        @pl.when(z > 0)
+        def _():
+            ag_copy(1, z, q).start()
+
+        @pl.when((z < n - 1) & (q < early))
+        def _():
+            ag_copy(0, z, q).start()
 
     def trade_start(i, carry):
         s, q = i // n_q, i % n_q
@@ -176,6 +180,16 @@
                     win_up(p).start()
                 for k in range(1, tiles):
                     win_side(p, k).start()
+
+    @pl.when((t == 0) & (z == 0))
+    def _():
+        for p in range(pieces):
+            win_up(p).wait_send()
+
+    for q in range(n_q):
+        @pl.when((z < n - 1) & (q >= early))
+        def _():
+            ag_copy(0, z, q).start()
 
     def inner_of(m):
         drow = jnp.broadcast_to(scales[m:m + 1, :], core.shape)
@@ -418,7 +432,7 @@
     @pl.when(t == 0)
     def _():
         for p in range(pieces):
-            @pl.when(z < n - 1)
+            @pl.when((z > 0) & (z < n - 1))
             def _():
                 win_up(p).wait_send()
             for k in range(1, tiles):

time: 105 us -> 101 us (0.962)
  Pallas kernels: 96.1 us -> 92.3 us
    pallas_call x1, Pallas kernels: 96.1 us -> 92.3 us  [fused(): pl.pallas_call(functools.partial(kernel, n, tiles, coef), out_shape=(jax....]
where the time goes in v4:
time: 101 us; the launch traced here: 99.7 us
  Pallas kernels  92.3 us (91%)
  local copies, waits for them, and re-layouts  6.74 us (7%)
    pallas_call x1, Pallas kernels, fused(): pl.pallas_call(functools.partial(kernel, n, tiles, coef), out_shape=(jax....  92.3 us
    unnamed x4, local copies, waits for them, and re-layouts  6.74 us

profile of v4, /device:TPU:25, one launch (start us, length us, event | category | flops | bytes accessed | tf_op | source)
XLA Modules:
  0.0 99.7 jit_solution(14056250617505543615)
XLA Ops:
  0.6 92.3 %shard_map.75 = (f32[1024,256]{1,0:T(8,128)}, f32[128,256]{1,0:T(8,128)}, f32[256,256]{1,0:T(8,128)}, f32[2,256]{1,0:T(2,128)}) custom-call(bf16[2,1,256,8192]{3,2,1,0:T(8,128)(2,1)} %trade.1, bf16[1024,256]{1,0:T(8,128)(2,1)} %factor.1, f32[2,256]{1,0:T(2,128)} %scales.1, f32[256,256]{1,0:T(8,128)} %core.1), custom_call_target="tpu_custom_call" | custom-call | tf_op jit(solution)/shard_map/pallas_call | solution.py:454
  93.0 2.3 %copy.12 = f32[1024,256]{1,0:T(8,128)} copy(f32[1024,256]{1,0:T(8,128)} %get-tuple-element.8) | data formatting | bytes 2097152
  95.2 1.6 %copy.13 = f32[128,256]{1,0:T(8,128)} copy(f32[128,256]{1,0:T(8,128)} %get-tuple-element.9) | data formatting | bytes 262144
  96.8 1.7 %copy.14 = f32[256,256]{1,0:T(8,128)} copy(f32[256,256]{1,0:T(8,128)} %get-tuple-element.10) | data formatting | bytes 524288
  98.5 1.2 %copy.15 = f32[2,256]{1,0:T(2,128)} copy(f32[2,256]{1,0:T(2,128)} %get-tuple-element.11) | data formatting | bytes 4096

commit v5 on v4

--- a/solution.py
+++ b/solution.py
@@ -269,32 +269,7 @@
         compute_step(s, q)
         reduce_step(s, q)
         return carry
-    lax.fori_loop(0, n * n_q, main_step, 0)
-
-    win_t = win32.T
-    window_sum = jnp.zeros((wsize, core.shape[1]), jnp.float32)
-    core_sum = jnp.zeros(core.shape, jnp.float32)
-    diags = []
-    for m in range(months):
-        drow = jnp.broadcast_to(scales[m:m + 1, :], core.shape)
-        dcol = drow.T
-        inner = dcol * core[...] * drow
-        window_sum += lax.dot_general(fmat[m], inner, (((1,), (1,)), ((), ())),
-                                      precision=HIGHEST, preferred_element_type=jnp.float32)
-        gram = jnp.dot(win_t, fmat[m], precision=HIGHEST, preferred_element_type=jnp.float32)
-        core_sum += dcol * gram * drow
-        weighted = gram * core[...]
-        by_row = jnp.sum(weighted.T * dcol, axis=0, keepdims=True)
-        by_col = jnp.sum(weighted * dcol, axis=0, keepdims=True)
-        diags.append(-coef * (by_row + by_col))
     wr, cr = wfin.shape[1], cfin.shape[2]
-    for k in range(tiles):
-        for i in range(n):
-            w0, c0 = (i * tiles + k) * wr, (i * tiles + k) * cr
-            part[k, i, pl.ds(0, wr), :] = -coef * window_sum[w0:w0 + wr]
-            part[k, i, pl.ds(wr, cr), :] = -coef * core_sum[c0:c0 + cr]
-    dbuf[t] = jnp.concatenate(
-        diags + [jnp.zeros((8 - months, core.shape[1]), jnp.float32)], 0)
 
     def peer_t(k):
         return lax.rem(t + k, tiles)
@@ -330,9 +305,39 @@
     def p5(k, who):
         return to_tile(wfin.at[who], wfin.at[who], p5_send, p5_recv, k, who)
 
-    for k in range(1, tiles):
-        p1(k, t).start()
-        pd(k, t).start()
+    def finish():
+        win_t = win32.T
+        window_sum = jnp.zeros((wsize, core.shape[1]), jnp.float32)
+        core_sum = jnp.zeros(core.shape, jnp.float32)
+        diags = []
+        for m in range(months):
+            drow = jnp.broadcast_to(scales[m:m + 1, :], core.shape)
+            dcol = drow.T
+            inner = dcol * core[...] * drow
+            window_sum += lax.dot_general(fmat[m], inner, (((1,), (1,)), ((), ())),
+                                          precision=HIGHEST, preferred_element_type=jnp.float32)
+            gram = jnp.dot(win_t, fmat[m], precision=HIGHEST, preferred_element_type=jnp.float32)
+            core_sum += dcol * gram * drow
+            weighted = gram * core[...]
+            by_row = jnp.sum(weighted.T * dcol, axis=0, keepdims=True)
+            by_col = jnp.sum(weighted * dcol, axis=0, keepdims=True)
+            diags.append(-coef * (by_row + by_col))
+        for k in range(tiles):
+            for i in range(n):
+                w0, c0 = (i * tiles + k) * wr, (i * tiles + k) * cr
+                part[k, i, pl.ds(0, wr), :] = -coef * window_sum[w0:w0 + wr]
+                part[k, i, pl.ds(wr, cr), :] = -coef * core_sum[c0:c0 + cr]
+        dbuf[t] = jnp.concatenate(
+            diags + [jnp.zeros((8 - months, core.shape[1]), jnp.float32)], 0)
+        for k in range(1, tiles):
+            p1(k, t).start()
+            pd(k, t).start()
+
+    done = 0
+    for last in range(n // 2, n):
+        lax.fori_loop(done * n_q, (last + 1) * n_q, main_step, 0)
+        done = last + 1
+        pl.when(jnp.maximum(z, n - 1 - z) == last)(finish)
 
     def small_second():
         for k in range(1, tiles):

time: 101 us -> 101 us (level)
  no operation moved by 1% of the time
where the time goes in v5:
time: 101 us
  Pallas kernels  93.3 us (92%)
  local copies, waits for them, and re-layouts  6.74 us (7%)
    pallas_call x1, Pallas kernels, fused(): pl.pallas_call(functools.partial(kernel, n, tiles, coef), out_shape=(jax....  93.3 us
    unnamed x4, local copies, waits for them, and re-layouts  6.74 us

profile of v5, /device:TPU:25, one launch (start us, length us, event | category | flops | bytes accessed | tf_op | source)
XLA Modules:
  0.0 100.6 jit_solution(17369282830389031696)
XLA Ops:
  0.6 93.3 %shard_map.75 = (f32[1024,256]{1,0:T(8,128)}, f32[128,256]{1,0:T(8,128)}, f32[256,256]{1,0:T(8,128)}, f32[2,256]{1,0:T(2,128)}) custom-call(bf16[2,1,256,8192]{3,2,1,0:T(8,128)(2,1)} %trade.1, bf16[1024,256]{1,0:T(8,128)(2,1)} %factor.1, f32[2,256]{1,0:T(2,128)} %scales.1, f32[256,256]{1,0:T(8,128)} %core.1), custom_call_target="tpu_custom_call" | custom-call | tf_op jit(solution)/shard_map/pallas_call | solution.py:459
  93.9 2.3 %copy.12 = f32[1024,256]{1,0:T(8,128)} copy(f32[1024,256]{1,0:T(8,128)} %get-tuple-element.8) | data formatting | bytes 2097152
  96.2 1.6 %copy.13 = f32[128,256]{1,0:T(8,128)} copy(f32[128,256]{1,0:T(8,128)} %get-tuple-element.9) | data formatting | bytes 262144
  97.7 1.7 %copy.14 = f32[256,256]{1,0:T(8,128)} copy(f32[256,256]{1,0:T(8,128)} %get-tuple-element.10) | data formatting | bytes 524288
  99.4 1.2 %copy.15 = f32[2,256]{1,0:T(2,128)} copy(f32[2,256]{1,0:T(2,128)} %get-tuple-element.11) | data formatting | bytes 4096

commit v6 on v4

--- a/solution.py
+++ b/solution.py
@@ -108,7 +108,7 @@
     @pl.when((t == 0) & (z == 0))
     def _():
         for p in range(pieces):
-            win[pl.ds(p * wrow, wrow), :] = fac[0, p]
+            win[pl.ds(p * wrow, wrow), :] = fac[0, p * wrow // r, pl.ds(p * wrow % r, wrow), :]
 
     @pl.when((t == 0) & (z == 0))
     def _():
@@ -445,7 +445,7 @@
     r = 256
     n_q = shard // r
     wsize = 2 * rows
-    pieces = wsize // r
+    pieces = wsize // 128
     wr, cr = wsize // (n * tiles), size // (n * tiles)
     coef = 1.0 / math.sqrt(months * n * wsize)
     vmem = pl.BlockSpec(memory_space=pltpu.VMEM)

time: 101 us -> 97.3 us (0.963)
  Pallas kernels: 92.3 us -> 89.6 us
    pallas_call x1, Pallas kernels: 92.3 us -> 89.6 us  [fused(): pl.pallas_call(functools.partial(kernel, n, tiles, coef), out_shape=(jax....]
where the time goes in v6:
time: 97.3 us; the launch traced here: 97 us
  Pallas kernels  89.6 us (92%)
  local copies, waits for them, and re-layouts  6.74 us (7%)
    pallas_call x1, Pallas kernels, fused(): pl.pallas_call(functools.partial(kernel, n, tiles, coef), out_shape=(jax....  89.6 us
    unnamed x4, local copies, waits for them, and re-layouts  6.74 us

profile of v6, /device:TPU:25, one launch (start us, length us, event | category | flops | bytes accessed | tf_op | source)
XLA Modules:
  0.0 97.0 jit_solution(16498518748434525184)
XLA Ops:
  0.6 89.6 %shard_map.75 = (f32[1024,256]{1,0:T(8,128)}, f32[128,256]{1,0:T(8,128)}, f32[256,256]{1,0:T(8,128)}, f32[2,256]{1,0:T(2,128)}) custom-call(bf16[2,1,256,8192]{3,2,1,0:T(8,128)(2,1)} %trade.1, bf16[1024,256]{1,0:T(8,128)(2,1)} %factor.1, f32[2,256]{1,0:T(2,128)} %scales.1, f32[256,256]{1,0:T(8,128)} %core.1), custom_call_target="tpu_custom_call" | custom-call | tf_op jit(solution)/shard_map/pallas_call | solution.py:454
  90.3 2.3 %copy.12 = f32[1024,256]{1,0:T(8,128)} copy(f32[1024,256]{1,0:T(8,128)} %get-tuple-element.8) | data formatting | bytes 2097152
  92.5 1.6 %copy.13 = f32[128,256]{1,0:T(8,128)} copy(f32[128,256]{1,0:T(8,128)} %get-tuple-element.9) | data formatting | bytes 262144
  94.1 1.7 %copy.14 = f32[256,256]{1,0:T(8,128)} copy(f32[256,256]{1,0:T(8,128)} %get-tuple-element.10) | data formatting | bytes 524288
  95.8 1.2 %copy.15 = f32[2,256]{1,0:T(2,128)} copy(f32[2,256]{1,0:T(2,128)} %get-tuple-element.11) | data formatting | bytes 4096
